TPU v7x, 128 devices: a whole 4x4x4 slice. The times are simulated.
128 devices in a mesh: row: 8 (over y_hi, z), col: 8 (over x, y_lo), depth: 2 (over core).
Axes of the slice: x: 4, y: 4 (y_hi: 2, y_lo: 2; y = y_hi * 2 + y_lo), z: 4, core: 2. Of those that a mesh axis runs over, the one named last changes fastest.
Arguments:
- lambdas: float32 [3200, 11264], P(('col', 'depth'), 'row'), may hold values from -0.109375 to 0.109375
- amplitudes: float32 [3200, 11264], P(('row', 'depth'), 'col'), may hold values from -6 to 6
- virt_irrep: int32 [1200], replicated, may hold values from 0 to 7
- ab_first: int32 [11264], P(('row', 'depth')), may hold values from 0 to 1199
- ab_second: int32 [11264], P(('row', 'depth')), may hold values from 0 to 1199
- cd_first: int32 [11264], P('col'), may hold values from 0 to 1199
- cd_second: int32 [11264], P('col'), may hold values from 0 to 1199
Outputs:
- density_tile: float32 [11264, 11264], P(('row', 'depth'), 'col')
Inputs may be any that keep to these rules, and one draw needn't show every extreme that they name: `virt_irrep`: irrep labels of the eight D2h irreps. `ab_first`: indices of virtual orbitals. `ab_second`: indices of virtual orbitals. `cd_first`: indices of virtual orbitals. `cd_second`: indices of virtual orbitals.
All inputs are finite; a program needn't handle non-finite values.
Results may differ from a plain program's by a relative error of at most 0.00007.
Values sent between devices are 32-bit elements; how exact they have to be, the bound alone decides.
A program may use at most 128 MiB of HBM per device.

v0:
```python
import jax
import jax.numpy as jnp
from jax import lax
from jax.sharding import PartitionSpec as P


def lookup(index, virt_irrep):
    table = jnp.arange(virt_irrep.shape[0], dtype=jnp.int32)
    match = index[:, None] == table[None, :]
    return jnp.sum(jnp.where(match, virt_irrep[None, :], 0), axis=1)


def pair_signs(first, second, virt_irrep):
    return jnp.where(lookup(first, virt_irrep) > lookup(second, virt_irrep), -1.0, 1.0).astype(
        jnp.float32
    )


def contract(left, right):
    return lax.dot_general(
        left,
        right,
        (((0,), (0,)), ((), ())),
        precision=lax.Precision.HIGHEST,
        preferred_element_type=jnp.float32,
    )


def on_device(lambdas, amplitudes, virt_irrep, ab_first, ab_second, cd_first, cd_second):
    amp_rows = lax.all_gather(amplitudes, "row", axis=0, tiled=True)
    partial_tile = contract(lax.all_gather(lambdas, "col", axis=0, tiled=True), amp_rows)
    gamma_sum = lax.psum_scatter(partial_tile, "depth", scatter_dimension=0, tiled=True)
    sign_ab = pair_signs(ab_first, ab_second, virt_irrep)
    sign_cd = pair_signs(cd_first, cd_second, virt_irrep)
    return gamma_sum * sign_ab[:, None] * sign_cd[None, :]


def solution(mesh):
    return jax.shard_map(
        on_device,
        mesh=mesh,
        in_specs=(
            P(("col", "depth"), "row"),
            P(("row", "depth"), "col"),
            P(),
            P(("row", "depth")),
            P(("row", "depth")),
            P("col"),
            P("col"),
        ),
        out_specs=P(("row", "depth"), "col"),
        check_vma=False,
    )
```

profile of v0, /device:TPU:1, one launch (start us, length us, event | category | flops | bytes accessed | tf_op | source)
XLA Modules:
  0.0 393.0 jit_solution(18430957527425891444)
XLA Ops:
  6.5 0.0 all-gather.3.cloned.1.call-start
  6.5 0.7 all-gather.3.cloned.1.call-update
  7.3 0.0 all-gather.5.cloned.1.call-start
  7.3 0.7 all-gather.5.cloned.1.call-update
  8.0 0.0 reduce-scatter.2.cloned.1.call-start
  8.1 184.2 %all-gather.3.cloned.1.call-done = f32[1600,1408]{1,0:T(8,128)} async-done(((f32[200,1408]{1,0:T(8,128)}), f32[1600,1408]{1,0:T(8,128)}) %all-gather.3.cloned.1.call-update) | async-done | bytes 9011216 | tf_op jit(solution)/shard_map/all_gather | solution.py:31
  192.2 118.0 %all-gather.5.cloned.1.call-done = f32[1600,1408]{1,0:T(8,128)} async-done(((f32[200,1408]{1,0:T(8,128)}), f32[1600,1408]{1,0:T(8,128)}) %all-gather.5.cloned.1.call-update) | async-done | bytes 9011216 | tf_op jit(solution)/shard_map/all_gather | solution.py:30
  310.3 53.8 %fusion = f32[1408,1408]{1,0:T(8,128)} fusion(f32[1600,1408]{1,0:T(8,128)} %all-gather.3.cloned.1.call-done, f32[1600,1408]{1,0:T(8,128)} %all-gather.5.cloned.1.call-done), kind=kOutput, calls=%fused_computation.11 | convolution fusion | flops 38063308800 | bytes 25952256 | tf_op jit(solution)/shard_map/dot_general | solution.py:20
  364.1 0.0 copy-start
  364.1 0.0 copy-start.3
  364.1 0.0 copy-start.4
  364.1 0.0 copy-start.1
  364.2 0.0 copy-start.2
  364.2 0.0 reduce-scatter.2.cloned.1.call-update
  364.2 0.6 copy-done
  364.8 0.0 copy-done.3
  364.8 0.0 copy-done.4
  364.9 1.2 select_reduce_fusion.2
  366.0 0.0 copy-done.1
  366.0 0.0 copy-done.2
  366.1 2.4 select_reduce_fusion
  368.5 13.6 %reduce-scatter.2.cloned.1.call-done = f32[704,1408]{1,0:T(8,128)} async-done(((f32[1408,1408]{1,0:T(8,128)}), f32[704,1408]{1,0:T(8,128)}) %reduce-scatter.2.cloned.1.call-update) | async-done | bytes 3964944 | tf_op jit(solution)/shard_map/reduce_scatter | solution.py:32
  382.1 4.4 %multiply_multiply_fusion = f32[704,1408]{1,0:T(8,128)} fusion(f32[704,1408]{1,0:T(8,128)} %reduce-scatter.2.cloned.1.call-done, f32[1408]{0:T(1024)S(1)} %compare_select_fusion, f32[704]{0:T(1024)S(1)} %compare_select_fusion.1), kind=kLoop, calls=%fused_computation.4 | loop fusion | flops 1982464 | bytes 7938304 | tf_op jit(solution)/shard_map/mul | solution.py:35
  (2 shorter events, 0.0 us)
Async XLA Ops:
  6.5 185.7 %all-gather.3.cloned.1.call-start = ((), (), s32[]{:S(2)}) async-start(), calls=%async_computation.1 | async-start | bytes 10137600 | tf_op jit(solution)/shard_map/all_gather | solution.py:31
  7.3 303.0 %all-gather.5.cloned.1.call-start = ((), (), s32[]{:S(2)}) async-start(), calls=%async_computation.2 | async-start | bytes 10137600 | tf_op jit(solution)/shard_map/all_gather | solution.py:30
  8.0 374.1 %reduce-scatter.2.cloned.1.call-start = ((), (), s32[]{:S(2)}) async-start(), calls=%async_computation.3 | async-start | bytes 11894784 | tf_op jit(solution)/shard_map/reduce_scatter | solution.py:32
  364.1 0.7 copy-start
  364.1 0.7 copy-start.3
  364.1 0.7 copy-start.4
  364.1 1.9 copy-start.1
  364.2 1.9 copy-start.2
Sparse Core Ops, SparseCore 0:
  9.0 183.2 all-gather.2
  194.6 115.6 all-gather.4
  364.3 17.7 reduce-scatter.1
where the time goes:
time: 393 us
  waiting for transfers between devices  317 us (81%)
  matrix products  53.8 us (14%)
  between operations  13.2 us (3%)
  other arithmetic  8.02 us (2%)
    all_gather x1, waiting for transfers between devices, on_device(): lax.all_gather(lambdas, 'col', axis=0, tiled=True)  184 us
    all_gather x1, waiting for transfers between devices, on_device(): amp_rows = lax.all_gather(amplitudes, 'row', axis=0, tiled=True)  118 us
    dot_general x1, matrix products, contract(): lax.dot_general(left, right, (((0,), (0,)), ((), ())), precision=lax.Prec...  53.8 us
    reduce_scatter x1, waiting for transfers between devices, on_device(): lax.psum_scatter(partial_tile, 'depth', scatter_dimension=0, tiled=True)  13.6 us
  transfers between devices with their start and end apart: 3, of which 3 were waited for; matrix products, arithmetic and copies ran while one was open for 1% of the time, Pallas kernels for 0%

commit v1 on v0

v1 whole, which is shorter than its diff:
```python
import functools

import jax
import jax.numpy as jnp
from jax import lax
from jax.experimental import pallas as pl
from jax.experimental.pallas import tpu as pltpu
from jax.sharding import PartitionSpec as P

MESH = pl.DeviceIdType.MESH
F32, BF16 = jnp.float32, jnp.bfloat16

CHUNKS, ROWS = 11, 16
LAST_ROWS = 24
LAST_AT = (0, 2, 5, 7)
SOURCES = 8
WIDTH = 1408
HALF = 704
HALF_LANES = 768
HALF_AT = 640


class Side:
    def __init__(self, own, buf, last, me, ring, plane, device, send, recv, last_send, last_recv, core):
        self.own, self.buf, self.last = own, buf, last
        self.me, self.ring, self.plane, self.device = me, ring, plane, device
        self.send, self.recv, self.last_send, self.last_recv = send, recv, last_send, last_recv
        self.core, self.way = core, 1 - 2 * core

    def rows(self, block):
        at = self.core * (SOURCES * ROWS) + block * ROWS
        return pl.ds(pl.multiple_of(at, ROWS), ROWS)

    def last_rows(self, block):
        at = self.core * (SOURCES * LAST_ROWS) + block * LAST_ROWS
        return pl.ds(pl.multiple_of(at, 8), LAST_ROWS)

    def put(self, j, block, target, kind, own=False):
        here = self.buf.at[j, self.rows(block)]
        src = self.own.at[pl.ds(pl.multiple_of(j * ROWS, ROWS), ROWS)] if own else here
        pltpu.make_async_remote_copy(
            src_ref=src,
            dst_ref=here,
            send_sem=self.send.at[j],
            recv_sem=self.recv.at[j, kind],
            device_id=self.device(target),
            device_id_type=MESH,
        ).start()

    def got(self, j, kind, count=1):
        part = self.buf.at[j, pl.ds(0, count * ROWS)]
        pltpu.make_async_copy(part, part, self.recv.at[j, kind]).wait()

    def sent(self, j):
        part = self.buf.at[j, pl.ds(0, 7 * ROWS)]
        pltpu.make_async_copy(part, part, self.send.at[j]).wait()

    def cross_own(self, j):
        self.put(j, self.me, self.plane(self.me), 0, own=True)

    def ring_own(self, j):
        self.put(j, self.me, self.ring(self.me, self.way), 1, own=True)
        self.put(j, self.me, self.ring(self.me, -self.way), 3, own=True)

    def ring_partner(self, j):
        self.got(j, 0)
        block = self.plane(self.me)
        self.put(j, block, self.ring(self.me, self.way), 2)
        self.put(j, block, self.ring(self.me, -self.way), 3)

    def pass_own(self, j):
        self.got(j, 1)
        self.put(j, self.ring(self.me, -self.way), self.ring(self.me, self.way), 3)

    def pass_partner(self, j):
        self.got(j, 2)
        block = self.plane(self.ring(self.me, -self.way))
        self.put(j, block, self.ring(self.me, self.way), 3)

    def put_last(self, block, target, kind, own=False):
        here = self.last.at[self.last_rows(block)]
        src = self.own.at[pl.ds(CHUNKS * ROWS, LAST_ROWS)] if own else here
        pltpu.make_async_remote_copy(
            src_ref=src,
            dst_ref=here,
            send_sem=self.last_send,
            recv_sem=self.last_recv.at[kind],
            device_id=self.device(target),
            device_id_type=MESH,
        ).start()

    def got_last(self, kind):
        part = self.last.at[pl.ds(0, LAST_ROWS)]
        pltpu.make_async_copy(part, part, self.last_recv.at[kind]).wait()

    def sent_last(self):
        part = self.last.at[pl.ds(0, 7 * LAST_ROWS)]
        pltpu.make_async_copy(part, part, self.last_send).wait()

    def ring_last(self):
        self.put_last(self.me, self.ring(self.me, self.way), 0, own=True)
        self.put_last(self.me, self.ring(self.me, -self.way), 1, own=True)

    def pass_last(self):
        self.got_last(0)
        self.put_last(self.ring(self.me, -self.way), self.ring(self.me, self.way), 2)

    def cross_last(self, step):
        if step >= 2:
            self.got_last(step - 1)
        offset = (0, -self.way, self.way, 2)[step]
        self.put_last(self.ring(self.me, offset), self.plane(self.me), 3 + step)


def kernel(
    lam, amp, out,
    lam_buf, amp_buf, lam_last, amp_last, left, right,
    local_sem, lam_send, amp_send, lam_recv, amp_recv, lam_last_send, amp_last_send, lam_last_recv, amp_last_recv,
    core_send, core_recv, core_last_send, core_last_recv,
):
    row, col, core = lax.axis_index("row"), lax.axis_index("col"), lax.axis_index("depth")

    lam_side = Side(
        lam, lam_buf, lam_last, col,
        lambda k, s: (k + 2 * s + 8) % 8,
        lambda k: k + 1 - 2 * (k % 2),
        lambda k: (row, k, core),
        lam_send, lam_recv, lam_last_send, lam_last_recv, core,
    )
    amp_side = Side(
        amp, amp_buf, amp_last, row,
        lambda k, s: k // 4 * 4 + (k + s + 4) % 4,
        lambda k: (k + 4) % 8,
        lambda k: (k, col, core),
        amp_send, amp_recv, amp_last_send, amp_last_recv, core,
    )
    sides = (lam_side, amp_side)
    other = (row, col, 1 - core)

    barrier = pltpu.get_barrier_semaphore()
    partners = [other]
    for side in sides:
        partners += [side.device(k) for k in (side.plane(side.me), side.ring(side.me, 1), side.ring(side.me, -1))]
    for partner in partners:
        pl.semaphore_signal(barrier, inc=1, device_id=partner, device_id_type=MESH)
    pl.semaphore_wait(barrier, len(partners))

    for side in sides:
        side.cross_own(0)
    for side in sides:
        side.ring_own(0)
    for side in sides:
        side.ring_last()
    for side in sides:
        side.cross_own(1)

    def lay(j, _):
        for i, side in enumerate(sides):
            src = side.own.at[pl.ds(pl.multiple_of(j * ROWS, ROWS), ROWS)]
            pltpu.make_async_copy(src, side.buf.at[j, side.rows(side.me)], local_sem.at[i]).start()
        return 0

    lax.fori_loop(0, CHUNKS, lay, 0)
    for i, side in enumerate(sides):
        src = side.own.at[pl.ds(CHUNKS * ROWS, LAST_ROWS)]
        pltpu.make_async_copy(src, side.last.at[side.last_rows(side.me)], local_sem.at[i]).start()
    out[...] = jnp.zeros_like(out)
    for i, side in enumerate(sides):
        pltpu.make_async_copy(side.own, side.own, local_sem.at[i]).wait()

    def lanes(of):
        return pl.ds(pl.multiple_of(HALF_AT * of, 128), HALF_LANES)

    def core_copies(lam_rows, amp_rows, send, recv):
        lam_part = lam_rows.at[:, lanes(1 - core)]
        return [
            pltpu.make_async_remote_copy(
                src_ref=part, dst_ref=part, send_sem=send.at[i], recv_sem=recv.at[i], device_id=other, device_id_type=MESH
            )
            for i, part in enumerate((lam_part, amp_rows))
        ]

    def share(j):
        mine = pl.ds(pl.multiple_of(core * (SOURCES * ROWS), 128), SOURCES * ROWS)
        return core_copies(lam_buf.at[j, mine], amp_buf.at[j, mine], core_send.at[j], core_recv.at[j])

    def share_last():
        mine = pl.ds(pl.multiple_of(core * (SOURCES * LAST_ROWS), 64), SOURCES * LAST_ROWS)
        return core_copies(lam_last.at[mine], amp_last.at[mine], core_last_send, core_last_recv)

    def multiply(lam_rows, amp_rows):
        depth = lam_rows.shape[0]
        l = lam_rows[:, lanes(core)].T
        l_hi = l.astype(BF16)
        l_lo = (l - l_hi.astype(F32)).astype(BF16)
        left[:, 0:depth] = l_hi
        left[:, depth : 2 * depth] = l_hi
        left[:, 2 * depth : 3 * depth] = l_lo
        a = amp_rows[...]
        a_hi = a.astype(BF16)
        a_lo = (a - a_hi.astype(F32)).astype(BF16)
        right[0:depth] = a_hi
        right[depth : 2 * depth] = a_lo
        right[2 * depth : 3 * depth] = a_hi
        mine = pl.ds(pl.multiple_of((HALF_LANES - HALF) * core, 64), HALF)
        out[...] += jnp.dot(left[mine, 0 : 3 * depth], right[0 : 3 * depth], preferred_element_type=F32)

    def tick(t, _):
        @pl.when(t + 2 < CHUNKS)
        def _():
            for side in sides:
                side.cross_own(t + 2)

        @pl.when(t + 1 < CHUNKS)
        def _():
            for side in sides:
                side.ring_own(t + 1)

        @pl.when(t < CHUNKS)
        def _():
            for side in sides:
                side.ring_partner(t)
            for side in sides:
                side.pass_own(t)

        @pl.when((t >= 1) & (t <= CHUNKS))
        def _():
            for side in sides:
                side.pass_partner(t - 1)

        @pl.when(t == 0)
        def _():
            for side in sides:
                side.pass_last()

        for step, at in enumerate(LAST_AT):

            @pl.when(t == at)
            def _(step=step):
                for side in sides:
                    side.cross_last(step)

        @pl.when((t >= 3) & (t < CHUNKS + 3))
        def _():
            for copy in share(t - 3):
                copy.wait_recv()
            multiply(lam_buf.at[t - 3], amp_buf.at[t - 3])

        @pl.when((t >= 2) & (t < CHUNKS + 2))
        def _():
            for side in sides:
                side.got(t - 2, 3, 4)
            for copy in share(t - 2):
                copy.start()

        @pl.when(t == CHUNKS)
        def _():
            for side in sides:
                for step in range(4):
                    side.got_last(3 + step)
            for copy in share_last():
                copy.start()

        @pl.when(t == CHUNKS + 1)
        def _():
            for copy in share_last():
                copy.wait_recv()
            multiply(lam_last, amp_last)

        @pl.when(t >= 3)
        def _():
            for side in sides:
                side.sent(t - 3)
            for copy in share(t - 3):
                copy.wait_send()

        return 0

    lax.fori_loop(0, CHUNKS + 3, tick, 0)
    for side in sides:
        side.sent_last()
    for copy in share_last():
        copy.wait_send()


def gather_multiply(lambdas, amplitudes):
    dma = pltpu.SemaphoreType.DMA
    return pl.pallas_call(
        kernel,
        out_shape=jax.ShapeDtypeStruct((HALF, WIDTH), F32),
        in_specs=[pl.BlockSpec(memory_space=pl.ANY)] * 2,
        out_specs=pl.BlockSpec(memory_space=pltpu.VMEM),
        scratch_shapes=[
            pltpu.VMEM((CHUNKS, 2 * SOURCES * ROWS, WIDTH), F32),
            pltpu.VMEM((CHUNKS, 2 * SOURCES * ROWS, WIDTH), F32),
            pltpu.VMEM((2 * SOURCES * LAST_ROWS, WIDTH), F32),
            pltpu.VMEM((2 * SOURCES * LAST_ROWS, WIDTH), F32),
            pltpu.VMEM((HALF_LANES, 3 * 2 * SOURCES * LAST_ROWS), BF16),
            pltpu.VMEM((3 * 2 * SOURCES * LAST_ROWS, WIDTH), BF16),
            dma((2,)),
            dma((CHUNKS,)),
            dma((CHUNKS,)),
            dma((CHUNKS, 4)),
            dma((CHUNKS, 4)),
            dma,
            dma,
            dma((7,)),
            dma((7,)),
            dma((CHUNKS, 2)),
            dma((CHUNKS, 2)),
            dma((2,)),
            dma((2,)),
        ],
        compiler_params=pltpu.CompilerParams(collective_id=0, has_side_effects=True, vmem_limit_bytes=58 << 20),
        cost_estimate=pl.CostEstimate(flops=6 * 3200 * HALF * WIDTH, bytes_accessed=8 << 20, transcendentals=0),
    )(lambdas, amplitudes)


def lookup(index, virt_irrep):
    table = jnp.arange(virt_irrep.shape[0], dtype=jnp.int32)
    match = index[:, None] == table[None, :]
    return jnp.sum(jnp.where(match, virt_irrep[None, :], 0), axis=1)


def pair_signs(first, second, virt_irrep):
    return jnp.where(lookup(first, virt_irrep) > lookup(second, virt_irrep), -1.0, 1.0).astype(F32)


def on_device(lambdas, amplitudes, virt_irrep, ab_first, ab_second, cd_first, cd_second):
    sign_ab = pair_signs(ab_first, ab_second, virt_irrep)
    sign_cd = pair_signs(cd_first, cd_second, virt_irrep)
    gamma_sum = gather_multiply(lambdas, amplitudes)
    return gamma_sum * sign_ab[:, None] * sign_cd[None, :]


def solution(mesh):
    return jax.shard_map(
        on_device,
        mesh=mesh,
        in_specs=(
            P(("col", "depth"), "row"),
            P(("row", "depth"), "col"),
            P(),
            P(("row", "depth")),
            P(("row", "depth")),
            P("col"),
            P("col"),
        ),
        out_specs=P(("row", "depth"), "col"),
        check_vma=False,
    )
```

time: 393 us -> 106 us (0.27)
  waiting for transfers between devices: 317 us -> 0 us
  Pallas kernels: 0 us -> 96.1 us
  matrix products: 53.8 us -> 0 us
  between operations: 13.2 us -> 0.03 us
    all_gather x2 -> x0, waiting for transfers between devices: 302 us -> none  [the longest x1 184 us: on_device(): lax.all_gather(lambdas, 'col', axis=0, tiled=True)]
    pallas_call x0 -> x1, Pallas kernels: none -> 96.1 us  [gather_multiply(): pl.pallas_call(kernel, out_shape=jax.ShapeDtypeStruct((HALF, WIDTH), F32)...]
    dot_general x1 -> x0, matrix products: 53.8 us -> none  [contract(): lax.dot_general(left, right, (((0,), (0,)), ((), ())), precision=lax.Prec...]
    reduce_scatter x1 -> x0, waiting for transfers between devices: 13.6 us -> none  [on_device(): lax.psum_scatter(partial_tile, 'depth', scatter_dimension=0, tiled=True)]
  transfers between devices with their start and end apart: 3 -> 0, of which waited for: 3 -> 0; matrix products, arithmetic and copies ran while one was open for 1% -> 0% of each run, Pallas kernels for 0% -> 0%
where the time goes in v1:
time: 106 us
  Pallas kernels  96.1 us (91%)
  other arithmetic  9.4 us (9%)
    pallas_call x1, Pallas kernels, gather_multiply(): pl.pallas_call(kernel, out_shape=jax.ShapeDtypeStruct((HALF, WIDTH), F32)...  96.1 us
    reduce_sum x2, other arithmetic, lookup(): return jnp.sum(jnp.where(match, virt_irrep[None, :], 0), axis=1)  4.95 us
    mul x1, other arithmetic, on_device(): return gamma_sum * sign_ab[:, None] * sign_cd[None, :]  4.45 us

profile of v1, /device:TPU:1, one launch (start us, length us, event | category | flops | bytes accessed | tf_op | source)
XLA Modules:
  0.0 105.5 jit_solution(3286379231649220351)
XLA Ops:
  0.0 1.9 %select_reduce_fusion.2 = (s32[704]{0:T(1024)S(1)}, s32[704]{0:T(1024)S(1)}) fusion(s32[704]{0:T(1024)} %param.11, s32[1200]{0:T(1024)} %param.9, s32[704]{0:T(1024)} %param.10), kind=kLoop, calls=%fused_computation.5 | loop fusion | flops 5067392 | bytes 16064 | tf_op jit(solution)/shard_map/reduce_sum | solution.py:322
  1.9 3.1 %select_reduce_fusion = (s32[1408]{0:T(1024)S(1)}, s32[1408]{0:T(1024)S(1)}) fusion(s32[1408]{0:T(1024)} %param.13, s32[1200]{0:T(1024)} %param.9, s32[1408]{0:T(1024)} %param.12), kind=kLoop, calls=%fused_computation | loop fusion | flops 10134784 | bytes 27328 | tf_op jit(solution)/shard_map/reduce_sum | solution.py:322
  5.0 96.1 %shard_map.73 = f32[704,1408]{1,0:T(8,128)} custom-call(f32[200,1408]{1,0:T(8,128)} %lam.1, f32[200,1408]{1,0:T(8,128)} %amp.1), custom_call_target="tpu_custom_call" | custom-call | flops 19031654400 | bytes 8388608 | tf_op jit(solution)/shard_map/pallas_call | solution.py:288
  101.1 4.4 %multiply_multiply_fusion = f32[704,1408]{1,0:T(8,128)} fusion(f32[704,1408]{1,0:T(8,128)} %shard_map.73, f32[1408]{0:T(1024)S(1)} %compare_select_fusion, f32[704]{0:T(1024)S(1)} %compare_select_fusion.1), kind=kLoop, calls=%fused_computation.4 | loop fusion | flops 1982464 | bytes 7938304 | tf_op jit(solution)/shard_map/mul | solution.py:333
  (2 shorter events, 0.0 us)

commit v2 on v0

v2 whole, which is shorter than its diff:
```python
import functools

import jax
import jax.numpy as jnp
from jax import lax
from jax.experimental import pallas as pl
from jax.experimental.pallas import tpu as pltpu
from jax.sharding import PartitionSpec as P

MESH = pl.DeviceIdType.MESH
F32, BF16, I32 = jnp.float32, jnp.bfloat16, jnp.int32

MAIN, MAIN_ROWS = 11, 16
SMALL, SMALL_ROWS = 1, 8
CHUNKS = MAIN + SMALL
LAST_ROWS = 16
LAST_AT = (0, 3, 6, 8)
LAST_SHARE, LAST_MULTIPLY = 10, 11
SOURCES = 8
WIDTH = 1408
HALF = 704
HALF_LANES = 768
HALF_AT = 640
ORBITALS = 1200
TABLE = 1280


class Chunk:
    def __init__(self, side, buf, rows, start, send, recv):
        self.side, self.buf, self.rows, self.start, self.send, self.recv = side, buf, rows, start, send, recv

    def at(self, block):
        first = (self.side.core * SOURCES + block) * self.rows
        return self.buf.at[pl.ds(pl.multiple_of(first, 8), self.rows)]

    def own(self):
        return self.side.own.at[pl.ds(pl.multiple_of(self.start, 8), self.rows)]

    def lay(self, sem):
        pltpu.make_async_copy(self.own(), self.at(self.side.me), sem).start()

    def put(self, block, target, kind, own=False):
        here = self.at(block)
        pltpu.make_async_remote_copy(
            src_ref=self.own() if own else here,
            dst_ref=here,
            send_sem=self.send,
            recv_sem=self.recv(kind),
            device_id=self.side.device(target),
            device_id_type=MESH,
        ).start()

    def wait(self, sem, blocks):
        part = self.buf.at[pl.ds(0, blocks * self.rows)]
        pltpu.make_async_copy(part, part, sem).wait()

    def got(self, kind, blocks=1):
        self.wait(self.recv(kind), blocks)

    def sent(self):
        self.wait(self.send, 7)

    def cross_own(self):
        self.put(self.side.me, self.side.plane(self.side.me), 0, own=True)

    def ring_own(self):
        side = self.side
        self.put(side.me, side.ring(side.me, side.way), 1, own=True)
        self.put(side.me, side.ring(side.me, -side.way), 3, own=True)

    def ring_partner(self):
        side = self.side
        self.got(0)
        block = side.plane(side.me)
        self.put(block, side.ring(side.me, side.way), 2)
        self.put(block, side.ring(side.me, -side.way), 3)

    def pass_own(self):
        side = self.side
        self.got(1)
        self.put(side.ring(side.me, -side.way), side.ring(side.me, side.way), 3)

    def pass_partner(self):
        side = self.side
        self.got(2)
        self.put(side.plane(side.ring(side.me, -side.way)), side.ring(side.me, side.way), 4)

    def ring_last(self):
        side = self.side
        self.put(side.me, side.ring(side.me, side.way), 0, own=True)
        self.put(side.me, side.ring(side.me, -side.way), 1, own=True)

    def pass_last(self):
        side = self.side
        self.got(0)
        self.put(side.ring(side.me, -side.way), side.ring(side.me, side.way), 2)

    def cross_last(self, step):
        side = self.side
        if step >= 2:
            self.got(step - 1)
        offset = (0, -side.way, side.way, 2)[step]
        self.put(side.ring(side.me, offset), side.plane(side.me), 3 + step)


class Side:
    def __init__(self, own, core, me, ring, plane, device):
        self.own, self.core, self.me = own, core, me
        self.ring, self.plane, self.device = ring, plane, device
        self.way = 1 - 2 * core


def set_signs(virt, first, second, row_out, table_col):
    tile = lax.broadcasted_iota(I32, (TABLE, 128), 0)
    full = first.shape[0]
    for at in range(0, full, 128):
        width = min(128, full - at)
        lanes = pl.ds(at, width)
        held = table_col[:, 0:width]
        rows = tile[:, 0:width]
        of_first = jnp.where(rows == first[lanes].reshape(1, width), held, 0.0)
        of_second = jnp.where(rows == second[lanes].reshape(1, width), held, 0.0)
        gap = jnp.sum(of_first - of_second, axis=0, keepdims=True)
        row_out[0:1, lanes] = jnp.where(gap > 0.0, -1.0, 1.0)


def kernel(
    lam, amp, virt, ab_first, ab_second, cd_first, cd_second, out,
    lam_main, amp_main, lam_small, amp_small, lam_last, amp_last, left, right,
    table_row, table_col, ab_row, ab_col, cd_row,
    local_sem, main_send, main_recv, small_send, small_recv, last_send, last_recv,
    core_send, core_recv, small_core_send, small_core_recv, last_core_send, last_core_recv,
):
    row, col, core = lax.axis_index("row"), lax.axis_index("col"), lax.axis_index("depth")
    lam_side = Side(
        lam, core, col,
        lambda k, s: (k + 2 * s + 8) % 8,
        lambda k: k + 1 - 2 * (k % 2),
        lambda k: (row, k, core),
    )
    amp_side = Side(
        amp, core, row,
        lambda k, s: k // 4 * 4 + (k + s + 4) % 4,
        lambda k: (k + 4) % 8,
        lambda k: (k, col, core),
    )
    sides = (lam_side, amp_side)
    other = (row, col, 1 - core)

    barrier = pltpu.get_barrier_semaphore()
    partners = [other]
    for side in sides:
        partners += [side.device(k) for k in (side.plane(side.me), side.ring(side.me, 1), side.ring(side.me, -1))]
    for partner in partners:
        pl.semaphore_signal(barrier, inc=1, device_id=partner, device_id_type=MESH)

    table_row[...] = jnp.zeros_like(table_row)
    table_row[0:1, 0:ORBITALS] = virt[...].astype(F32).reshape(1, ORBITALS)
    table_col[...] = jnp.broadcast_to(table_row[0:1, :], (128, TABLE)).T
    ab_row[...] = jnp.ones_like(ab_row)
    set_signs(virt, ab_first, ab_second, ab_row, table_col)
    set_signs(virt, cd_first, cd_second, cd_row, table_col)
    shifted = pltpu.roll(ab_row[...], (HALF_LANES - HALF) * core, 1)
    ab_col[...] = jnp.broadcast_to(shifted[0:1, :], (128, HALF_LANES)).T
    out[...] = jnp.zeros_like(out)
    pl.semaphore_wait(barrier, len(partners))

    def main(j):
        return [
            Chunk(side, buf.at[j], MAIN_ROWS, j * MAIN_ROWS, main_send.at[i, j], lambda k, i=i: main_recv.at[i, j, k])
            for i, (side, buf) in enumerate(zip(sides, (lam_main, amp_main)))
        ]

    def small(j):
        start = MAIN * MAIN_ROWS + j * SMALL_ROWS
        return [
            Chunk(side, buf.at[j], SMALL_ROWS, start, small_send.at[i, j], lambda k, i=i: small_recv.at[i, j, k])
            for i, (side, buf) in enumerate(zip(sides, (lam_small, amp_small)))
        ]

    start = MAIN * MAIN_ROWS + SMALL * SMALL_ROWS
    last = [
        Chunk(side, buf, LAST_ROWS, start, last_send.at[i], lambda k, i=i: last_recv.at[i, k])
        for i, (side, buf) in enumerate(zip(sides, (lam_last, amp_last)))
    ]

    def on_chunk(j, do):
        @pl.when((j >= 0) & (j < MAIN))
        def _():
            for chunk in main(j):
                do(chunk)

        @pl.when((j >= MAIN) & (j < CHUNKS))
        def _():
            for chunk in small(j - MAIN):
                do(chunk)

    for chunk in main(0):
        chunk.cross_own()
    for chunk in main(0):
        chunk.ring_own()
    for chunk in last:
        chunk.ring_last()
    for chunk in main(1):
        chunk.cross_own()

    def lay(j, _):
        for i, chunk in enumerate(main(j)):
            chunk.lay(local_sem.at[i])
        return 0

    lax.fori_loop(0, MAIN, lay, 0)
    for j in range(SMALL):
        for i, chunk in enumerate(small(j)):
            chunk.lay(local_sem.at[i])
    for i, chunk in enumerate(last):
        chunk.lay(local_sem.at[i])
    for i, side in enumerate(sides):
        pltpu.make_async_copy(side.own, side.own, local_sem.at[i]).wait()

    def lanes(of):
        return pl.ds(pl.multiple_of(HALF_AT * of, 128), HALF_LANES)

    def to_core(parts, send, recv):
        return [
            pltpu.make_async_remote_copy(
                src_ref=part, dst_ref=part, send_sem=send.at[i], recv_sem=recv.at[i], device_id=other, device_id_type=MESH
            )
            for i, part in enumerate(parts)
        ]

    def share(chunks, send, recv):
        lam_chunk, amp_chunk = chunks
        rows = SOURCES * lam_chunk.rows
        mine = pl.ds(pl.multiple_of(core * rows, 64), rows)
        return to_core((lam_chunk.buf.at[mine, lanes(1 - core)], amp_chunk.buf.at[mine]), send, recv)

    def share_main(j):
        return share(main(j), core_send.at[j], core_recv.at[j])

    def share_last():
        return share(last, last_core_send, last_core_recv)

    def share_block(chunks, block_of, send, recv):
        lam_chunk, amp_chunk = chunks
        parts = (lam_chunk.at(block_of(lam_side)).at[:, lanes(1 - core)], amp_chunk.at(block_of(amp_side)))
        return to_core(parts, send, recv)

    def far(side):
        return side.plane(side.ring(side.me, 2))

    def share_early(j):
        copies = []
        for s in (0, 1, -1, 2):
            copies += share_block(small(j), lambda side: side.ring(side.me, s), small_core_send.at[j], small_core_recv.at[j, 0])
            if s != 2:
                copies += share_block(
                    small(j), lambda side: side.plane(side.ring(side.me, s)), small_core_send.at[j], small_core_recv.at[j, 0]
                )
        return copies

    def share_far(j):
        return share_block(small(j), far, small_core_send.at[j], small_core_recv.at[j, 1])

    def small_wait(j, sem, blocks):
        lam_chunk, amp_chunk = small(j)
        rows = pl.ds(0, blocks * SMALL_ROWS)
        for i, part in enumerate((lam_chunk.buf.at[rows, lanes(0)], amp_chunk.buf.at[rows])):
            pltpu.make_async_copy(part, part, sem.at[i]).wait()

    def multiply(lam_rows, amp_rows):
        depth = lam_rows.shape[0]
        l = lam_rows[:, lanes(core)].T * jnp.concatenate([ab_col[...]] * (depth // 128), axis=1)
        l_hi = l.astype(BF16)
        l_lo = (l - l_hi.astype(F32)).astype(BF16)
        left[:, 0:depth] = l_hi
        left[:, depth : 2 * depth] = l_hi
        left[:, 2 * depth : 3 * depth] = l_lo
        a = amp_rows[...] * cd_row[0:1, :]
        a_hi = a.astype(BF16)
        a_lo = (a - a_hi.astype(F32)).astype(BF16)
        right[0:depth] = a_hi
        right[depth : 2 * depth] = a_lo
        right[2 * depth : 3 * depth] = a_hi
        mine = pl.ds(pl.multiple_of((HALF_LANES - HALF) * core, 64), HALF)
        out[...] += jnp.dot(left[mine, 0 : 3 * depth], right[0 : 3 * depth], preferred_element_type=F32)

    def tick(t, _):
        on_chunk(t + 2, lambda chunk: chunk.cross_own())
        on_chunk(t + 1, lambda chunk: chunk.ring_own())
        on_chunk(t, lambda chunk: chunk.ring_partner())
        on_chunk(t, lambda chunk: chunk.pass_own())
        on_chunk(t - 1, lambda chunk: chunk.pass_partner())

        @pl.when(t == 0)
        def _():
            for chunk in last:
                chunk.pass_last()

        for step, at in enumerate(LAST_AT):

            @pl.when(t == at)
            def _(step=step):
                for chunk in last:
                    chunk.cross_last(step)

        @pl.when((t >= 3) & (t < MAIN + 3))
        def _():
            for copy in share_main(t - 3):
                copy.wait_recv()
            multiply(lam_main.at[t - 3], amp_main.at[t - 3])

        @pl.when((t >= 2) & (t < MAIN + 2))
        def _():
            for chunk in main(t - 2):
                chunk.got(3, 3)
                chunk.got(4)
            for copy in share_main(t - 2):
                copy.start()

        @pl.when(t == LAST_SHARE)
        def _():
            for chunk in last:
                for step in range(4):
                    chunk.got(3 + step)
            for copy in share_last():
                copy.start()

        @pl.when(t == LAST_MULTIPLY)
        def _():
            for copy in share_last():
                copy.wait_recv()
            multiply(lam_last, amp_last)

        @pl.when((t >= MAIN + 1) & (t < CHUNKS + 1))
        def _():
            j = t - 1 - MAIN
            for chunk in small(j):
                chunk.got(3, 3)
            for copy in share_early(j):
                copy.start()

        @pl.when((t >= MAIN + 2) & (t < CHUNKS + 2))
        def _():
            j = t - 2 - MAIN
            for chunk in small(j):
                chunk.got(4)
            for copy in share_far(j):
                copy.start()
            small_wait(j, small_core_recv.at[j, 0], 7)
            small_wait(j, small_core_recv.at[j, 1], 1)
            multiply(lam_small.at[j], amp_small.at[j])

        @pl.when((t >= 3) & (t < MAIN + 3))
        def _():
            for chunk in main(t - 3):
                chunk.sent()
            for copy in share_main(t - 3):
                copy.wait_send()

        return 0

    lax.fori_loop(0, max(CHUNKS + 2, MAIN + 3), tick, 0)
    for j in range(SMALL):
        for chunk in small(j):
            chunk.sent()
        small_wait(j, small_core_send.at[j], 8)
    for chunk in last:
        chunk.sent()
    for copy in share_last():
        copy.wait_send()


def gather_multiply(lambdas, amplitudes, virt_irrep, ab_first, ab_second, cd_first, cd_second):
    dma = pltpu.SemaphoreType.DMA
    most = 3 * 2 * SOURCES * max(MAIN_ROWS, SMALL_ROWS, LAST_ROWS)
    rows = [virt_irrep, ab_first, ab_second, cd_first, cd_second]
    buffers = [
        pltpu.VMEM(shape, F32)
        for shape in (
            (MAIN, 2 * SOURCES * MAIN_ROWS, WIDTH),
            (SMALL, 2 * SOURCES * SMALL_ROWS, WIDTH),
            (2 * SOURCES * LAST_ROWS, WIDTH),
        )
        for _ in range(2)
    ]
    return pl.pallas_call(
        kernel,
        out_shape=pltpu.VMEM((HALF, WIDTH), F32),
        in_specs=[pl.BlockSpec(memory_space=pl.ANY)] * 2 + [pl.BlockSpec(memory_space=pltpu.VMEM)] * 5,
        out_specs=pl.BlockSpec(memory_space=pltpu.VMEM),
        scratch_shapes=buffers
        + [
            pltpu.VMEM((HALF_LANES, most), BF16),
            pltpu.VMEM((most, WIDTH), BF16),
            pltpu.VMEM((8, TABLE), F32),
            pltpu.VMEM((TABLE, 128), F32),
            pltpu.VMEM((8, HALF_LANES), F32),
            pltpu.VMEM((HALF_LANES, 128), F32),
            pltpu.VMEM((8, WIDTH), F32),
            dma((2,)),
            dma((2, MAIN)),
            dma((2, MAIN, 5)),
            dma((2, SMALL)),
            dma((2, SMALL, 5)),
            dma((2,)),
            dma((2, 7)),
            dma((MAIN, 2)),
            dma((MAIN, 2)),
            dma((SMALL, 2)),
            dma((SMALL, 2, 2)),
            dma((2,)),
            dma((2,)),
        ],
        compiler_params=pltpu.CompilerParams(collective_id=0, has_side_effects=True, vmem_limit_bytes=54 << 20),
        cost_estimate=pl.CostEstimate(flops=6 * 3200 * HALF * WIDTH, bytes_accessed=8 << 20, transcendentals=0),
    )(lambdas, amplitudes, *rows)


def solution(mesh):
    return jax.shard_map(
        gather_multiply,
        mesh=mesh,
        in_specs=(
            P(("col", "depth"), "row"),
            P(("row", "depth"), "col"),
            P(),
            P(("row", "depth")),
            P(("row", "depth")),
            P("col"),
            P("col"),
        ),
        out_specs=P(("row", "depth"), "col"),
        check_vma=False,
    )
```

time: 393 us -> 95.9 us (0.24)
  waiting for transfers between devices: 317 us -> 0 us
  Pallas kernels: 0 us -> 93.7 us
  matrix products: 53.8 us -> 0 us
  between operations: 13.2 us -> 0.01 us
  other arithmetic: 8.02 us -> 0 us
    all_gather x2 -> x0, waiting for transfers between devices: 302 us -> none  [the longest x1 184 us: on_device(): lax.all_gather(lambdas, 'col', axis=0, tiled=True)]
    pallas_call x0 -> x1, Pallas kernels: none -> 93.7 us  [gather_multiply(): pl.pallas_call(kernel, out_shape=pltpu.VMEM((HALF, WIDTH), F32), in_specs...]
    dot_general x1 -> x0, matrix products: 53.8 us -> none  [contract(): lax.dot_general(left, right, (((0,), (0,)), ((), ())), precision=lax.Prec...]
    reduce_scatter x1 -> x0, waiting for transfers between devices: 13.6 us -> none  [on_device(): lax.psum_scatter(partial_tile, 'depth', scatter_dimension=0, tiled=True)]
    mul x1 -> x0, other arithmetic: 4.44 us -> none  [on_device(): return gamma_sum * sign_ab[:, None] * sign_cd[None, :]]
  transfers between devices with their start and end apart: 3 -> 0, of which waited for: 3 -> 0; matrix products, arithmetic and copies ran while one was open for 1% -> 0% of each run, Pallas kernels for 0% -> 0%
where the time goes in v2:
time: 95.9 us; the launch traced here: 95.7 us
  Pallas kernels  93.7 us (98%)
  local copies, waits for them, and re-layouts  1.94 us (2%)
    pallas_call x1, Pallas kernels, gather_multiply(): pl.pallas_call(kernel, out_shape=pltpu.VMEM((HALF, WIDTH), F32), in_specs...  93.7 us
    unnamed x1, local copies, waits for them, and re-layouts  1.94 us

profile of v2, /device:TPU:1, one launch (start us, length us, event | category | flops | bytes accessed | tf_op | source)
XLA Modules:
  0.0 95.7 jit_solution(13235692700543444237)
XLA Ops:
  0.0 93.7 %shard_map.73 = f32[704,1408]{1,0:T(8,128)S(1)} custom-call(f32[200,1408]{1,0:T(8,128)} %lam.1, f32[200,1408]{1,0:T(8,128)} %amp.1, s32[1200]{0:T(1024)} %virt.1, s32[704]{0:T(1024)} %ab_first.1, s32[704]{0:T(1024)} %ab_second.1, s32[1408]{0:T(1024)} %cd_first.1, s32[1408]{0:T(1024)} %cd_second.1), custom_call_target="tpu_custom_call" | custom-call | flops 19031654400 | bytes 8388608 | tf_op jit(solution)/shard_map/pallas_call | solution.py:387
  93.8 1.9 %copy.9 = f32[704,1408]{1,0:T(8,128)} copy(f32[704,1408]{1,0:T(8,128)S(1)} %shard_map.73) | data formatting | bytes 7929856

commit v3 on v2

--- a/solution.py
+++ b/solution.py
@@ -14,8 +14,9 @@
 SMALL, SMALL_ROWS = 1, 8
 CHUNKS = MAIN + SMALL
 LAST_ROWS = 16
-LAST_AT = (0, 3, 6, 8)
-LAST_SHARE, LAST_MULTIPLY = 10, 11
+LAST_AT = (0, 2, 4, 7)
+LAST_SHARE, LAST_MULTIPLY = 9, 10
+SHARE_LAG = 3
 SOURCES = 8
 WIDTH = 1408
 HALF = 704
@@ -61,53 +62,56 @@
         self.wait(self.send, 7)
 
     def cross_own(self):
-        self.put(self.side.me, self.side.plane(self.side.me), 0, own=True)
+        self.put(self.side.me, self.side.pair, 0, own=True)
 
     def ring_own(self):
         side = self.side
-        self.put(side.me, side.ring(side.me, side.way), 1, own=True)
-        self.put(side.me, side.ring(side.me, -side.way), 3, own=True)
+        self.put(side.me, side.ahead, 1, own=True)
+        self.put(side.me, side.behind, 3, own=True)
 
     def ring_partner(self):
         side = self.side
         self.got(0)
-        block = side.plane(side.me)
-        self.put(block, side.ring(side.me, side.way), 2)
-        self.put(block, side.ring(side.me, -side.way), 3)
+        block = side.pair
+        self.put(block, side.ahead, 2)
+        self.put(block, side.behind, 3)
 
     def pass_own(self):
         side = self.side
         self.got(1)
-        self.put(side.ring(side.me, -side.way), side.ring(side.me, side.way), 3)
+        self.put(side.behind, side.ahead, 3)
 
     def pass_partner(self):
         side = self.side
         self.got(2)
-        self.put(side.plane(side.ring(side.me, -side.way)), side.ring(side.me, side.way), 4)
+        self.put(side.pair_behind, side.ahead, 4)
 
     def ring_last(self):
         side = self.side
-        self.put(side.me, side.ring(side.me, side.way), 0, own=True)
-        self.put(side.me, side.ring(side.me, -side.way), 1, own=True)
+        self.put(side.me, side.ahead, 0, own=True)
+        self.put(side.me, side.behind, 1, own=True)
 
     def pass_last(self):
         side = self.side
         self.got(0)
-        self.put(side.ring(side.me, -side.way), side.ring(side.me, side.way), 2)
+        self.put(side.behind, side.ahead, 2)
 
     def cross_last(self, step):
         side = self.side
         if step >= 2:
             self.got(step - 1)
-        offset = (0, -side.way, side.way, 2)[step]
-        self.put(side.ring(side.me, offset), side.plane(side.me), 3 + step)
+        block = (side.me, side.behind, side.ahead, side.opposite)[step]
+        self.put(block, side.pair, 3 + step)
 
 
 class Side:
     def __init__(self, own, core, me, ring, plane, device):
         self.own, self.core, self.me = own, core, me
-        self.ring, self.plane, self.device = ring, plane, device
-        self.way = 1 - 2 * core
+        self.device = device
+        way = 1 - 2 * core
+        self.ahead, self.behind, self.opposite = ring(me, way), ring(me, -way), ring(me, 2)
+        self.pair, self.pair_ahead, self.pair_behind = plane(me), plane(self.ahead), plane(self.behind)
+        self.far = plane(self.opposite)
 
 
 def set_signs(virt, first, second, row_out, table_col):
@@ -125,7 +129,8 @@
 
 
 def kernel(
-    lam, amp, virt, ab_first, ab_second, cd_first, cd_second, out,
+    lam, amp, virt_in, ab_first_in, ab_second_in, cd_first_in, cd_second_in, out,
+    virt, ab_first, ab_second, cd_first, cd_second,
     lam_main, amp_main, lam_small, amp_small, lam_last, amp_last, left, right,
     table_row, table_col, ab_row, ab_col, cd_row,
     local_sem, main_send, main_recv, small_send, small_recv, last_send, last_recv,
@@ -150,10 +155,78 @@
     barrier = pltpu.get_barrier_semaphore()
     partners = [other]
     for side in sides:
-        partners += [side.device(k) for k in (side.plane(side.me), side.ring(side.me, 1), side.ring(side.me, -1))]
+        partners += [side.device(k) for k in (side.pair, side.ahead, side.behind)]
     for partner in partners:
         pl.semaphore_signal(barrier, inc=1, device_id=partner, device_id_type=MESH)
 
+    staged = [
+        pltpu.make_async_copy(src, dst, local_sem.at[2 + i])
+        for i, (src, dst) in enumerate(
+            (
+                (virt_in, virt),
+                (ab_first_in, ab_first),
+                (ab_second_in, ab_second),
+                (cd_first_in, cd_first),
+                (cd_second_in, cd_second),
+            )
+        )
+    ]
+    for copy in staged:
+        copy.start()
+    pl.semaphore_wait(barrier, len(partners))
+
+    def main(j):
+        return [
+            Chunk(side, buf.at[j], MAIN_ROWS, j * MAIN_ROWS, main_send.at[i, j], lambda k, i=i: main_recv.at[i, j, k])
+            for i, (side, buf) in enumerate(zip(sides, (lam_main, amp_main)))
+        ]
+
+    def small(j):
+        start = MAIN * MAIN_ROWS + j * SMALL_ROWS
+        return [
+            Chunk(side, buf.at[j], SMALL_ROWS, start, small_send.at[i, j], lambda k, i=i: small_recv.at[i, j, k])
+            for i, (side, buf) in enumerate(zip(sides, (lam_small, amp_small)))
+        ]
+
+    start = MAIN * MAIN_ROWS + SMALL * SMALL_ROWS
+    last = [
+        Chunk(side, buf, LAST_ROWS, start, last_send.at[i], lambda k, i=i: last_recv.at[i, k])
+        for i, (side, buf) in enumerate(zip(sides, (lam_last, amp_last)))
+    ]
+
+    def on_chunk(j, do):
+        @pl.when((j >= 0) & (j < MAIN))
+        def _():
+            for chunk in main(j):
+                do(chunk)
+
+        @pl.when((j >= MAIN) & (j < CHUNKS))
+        def _():
+            for chunk in small(j - MAIN):
+                do(chunk)
+
+    for chunk in main(0):
+        chunk.cross_own()
+    for chunk in main(0):
+        chunk.ring_own()
+    for chunk in last:
+        chunk.ring_last()
+    for chunk in main(1):
+        chunk.cross_own()
+
+    def lay(j, _):
+        for i, chunk in enumerate(main(j)):
+            chunk.lay(local_sem.at[i])
+        return 0
+
+    lax.fori_loop(0, MAIN, lay, 0)
+    for j in range(SMALL):
+        for i, chunk in enumerate(small(j)):
+            chunk.lay(local_sem.at[i])
+    for i, chunk in enumerate(last):
+        chunk.lay(local_sem.at[i])
+    for copy in staged:
+        copy.wait()
     table_row[...] = jnp.zeros_like(table_row)
     table_row[0:1, 0:ORBITALS] = virt[...].astype(F32).reshape(1, ORBITALS)
     table_col[...] = jnp.broadcast_to(table_row[0:1, :], (128, TABLE)).T
@@ -163,58 +236,6 @@
     shifted = pltpu.roll(ab_row[...], (HALF_LANES - HALF) * core, 1)
     ab_col[...] = jnp.broadcast_to(shifted[0:1, :], (128, HALF_LANES)).T
     out[...] = jnp.zeros_like(out)
-    pl.semaphore_wait(barrier, len(partners))
-
-    def main(j):
-        return [
-            Chunk(side, buf.at[j], MAIN_ROWS, j * MAIN_ROWS, main_send.at[i, j], lambda k, i=i: main_recv.at[i, j, k])
-            for i, (side, buf) in enumerate(zip(sides, (lam_main, amp_main)))
-        ]
-
-    def small(j):
-        start = MAIN * MAIN_ROWS + j * SMALL_ROWS
-        return [
-            Chunk(side, buf.at[j], SMALL_ROWS, start, small_send.at[i, j], lambda k, i=i: small_recv.at[i, j, k])
-            for i, (side, buf) in enumerate(zip(sides, (lam_small, amp_small)))
-        ]
-
-    start = MAIN * MAIN_ROWS + SMALL * SMALL_ROWS
-    last = [
-        Chunk(side, buf, LAST_ROWS, start, last_send.at[i], lambda k, i=i: last_recv.at[i, k])
-        for i, (side, buf) in enumerate(zip(sides, (lam_last, amp_last)))
-    ]
-
-    def on_chunk(j, do):
-        @pl.when((j >= 0) & (j < MAIN))
-        def _():
-            for chunk in main(j):
-                do(chunk)
-
-        @pl.when((j >= MAIN) & (j < CHUNKS))
-        def _():
-            for chunk in small(j - MAIN):
-                do(chunk)
-
-    for chunk in main(0):
-        chunk.cross_own()
-    for chunk in main(0):
-        chunk.ring_own()
-    for chunk in last:
-        chunk.ring_last()
-    for chunk in main(1):
-        chunk.cross_own()
-
-    def lay(j, _):
-        for i, chunk in enumerate(main(j)):
-            chunk.lay(local_sem.at[i])
-        return 0
-
-    lax.fori_loop(0, MAIN, lay, 0)
-    for j in range(SMALL):
-        for i, chunk in enumerate(small(j)):
-            chunk.lay(local_sem.at[i])
-    for i, chunk in enumerate(last):
-        chunk.lay(local_sem.at[i])
     for i, side in enumerate(sides):
         pltpu.make_async_copy(side.own, side.own, local_sem.at[i]).wait()
 
@@ -247,16 +268,12 @@
         return to_core(parts, send, recv)
 
     def far(side):
-        return side.plane(side.ring(side.me, 2))
+        return side.far
 
     def share_early(j):
         copies = []
-        for s in (0, 1, -1, 2):
-            copies += share_block(small(j), lambda side: side.ring(side.me, s), small_core_send.at[j], small_core_recv.at[j, 0])
-            if s != 2:
-                copies += share_block(
-                    small(j), lambda side: side.plane(side.ring(side.me, s)), small_core_send.at[j], small_core_recv.at[j, 0]
-                )
+        for name in ("me", "ahead", "behind", "opposite", "pair", "pair_ahead", "pair_behind"):
+            copies += share_block(small(j), lambda side, name=name: getattr(side, name), small_core_send.at[j], small_core_recv.at[j, 0])
         return copies
 
     def share_far(j):
@@ -290,7 +307,20 @@
         on_chunk(t + 1, lambda chunk: chunk.ring_own())
         on_chunk(t, lambda chunk: chunk.ring_partner())
         on_chunk(t, lambda chunk: chunk.pass_own())
-        on_chunk(t - 1, lambda chunk: chunk.pass_partner())
+
+        @pl.when(t < CHUNKS)
+        def _():
+            on_chunk(t - 2, lambda chunk: chunk.pass_partner())
+
+        @pl.when(t == CHUNKS - 1)
+        def _():
+            for chunk in main(MAIN - 1):
+                chunk.pass_partner()
+
+        @pl.when(t == CHUNKS)
+        def _():
+            for chunk in small(SMALL - 1):
+                chunk.pass_partner()
 
         @pl.when(t == 0)
         def _():
@@ -303,20 +333,6 @@
             def _(step=step):
                 for chunk in last:
                     chunk.cross_last(step)
-
-        @pl.when((t >= 3) & (t < MAIN + 3))
-        def _():
-            for copy in share_main(t - 3):
-                copy.wait_recv()
-            multiply(lam_main.at[t - 3], amp_main.at[t - 3])
-
-        @pl.when((t >= 2) & (t < MAIN + 2))
-        def _():
-            for chunk in main(t - 2):
-                chunk.got(3, 3)
-                chunk.got(4)
-            for copy in share_main(t - 2):
-                copy.start()
 
         @pl.when(t == LAST_SHARE)
         def _():
@@ -332,35 +348,48 @@
                 copy.wait_recv()
             multiply(lam_last, amp_last)
 
-        @pl.when((t >= MAIN + 1) & (t < CHUNKS + 1))
-        def _():
-            j = t - 1 - MAIN
+        @pl.when((t >= SHARE_LAG) & (t < MAIN + SHARE_LAG))
+        def _():
+            j = t - SHARE_LAG
+            for chunk in main(j):
+                chunk.got(3, 3)
+                chunk.got(4)
+            for copy in share_main(j):
+                copy.start()
+
+        @pl.when((t >= MAIN + SHARE_LAG) & (t < CHUNKS + SHARE_LAG))
+        def _():
+            j = t - SHARE_LAG - MAIN
             for chunk in small(j):
                 chunk.got(3, 3)
             for copy in share_early(j):
                 copy.start()
-
-        @pl.when((t >= MAIN + 2) & (t < CHUNKS + 2))
-        def _():
-            j = t - 2 - MAIN
             for chunk in small(j):
                 chunk.got(4)
             for copy in share_far(j):
                 copy.start()
+
+        @pl.when((t >= SHARE_LAG + 1) & (t < MAIN + SHARE_LAG + 1))
+        def _():
+            j = t - SHARE_LAG - 1
+            for copy in share_main(j):
+                copy.wait_recv()
+            multiply(lam_main.at[j], amp_main.at[j])
+            for chunk in main(j):
+                chunk.sent()
+            for copy in share_main(j):
+                copy.wait_send()
+
+        @pl.when((t >= MAIN + SHARE_LAG + 1) & (t < CHUNKS + SHARE_LAG + 1))
+        def _():
+            j = t - SHARE_LAG - 1 - MAIN
             small_wait(j, small_core_recv.at[j, 0], 7)
             small_wait(j, small_core_recv.at[j, 1], 1)
             multiply(lam_small.at[j], amp_small.at[j])
 
-        @pl.when((t >= 3) & (t < MAIN + 3))
-        def _():
-            for chunk in main(t - 3):
-                chunk.sent()
-            for copy in share_main(t - 3):
-                copy.wait_send()
-
         return 0
 
-    lax.fori_loop(0, max(CHUNKS + 2, MAIN + 3), tick, 0)
+    lax.fori_loop(0, CHUNKS + SHARE_LAG + 1, tick, 0)
     for j in range(SMALL):
         for chunk in small(j):
             chunk.sent()
@@ -387,9 +416,10 @@
     return pl.pallas_call(
         kernel,
         out_shape=pltpu.VMEM((HALF, WIDTH), F32),
-        in_specs=[pl.BlockSpec(memory_space=pl.ANY)] * 2 + [pl.BlockSpec(memory_space=pltpu.VMEM)] * 5,
+        in_specs=[pl.BlockSpec(memory_space=pl.ANY)] * 7,
         out_specs=pl.BlockSpec(memory_space=pltpu.VMEM),
-        scratch_shapes=buffers
+        scratch_shapes=[pltpu.VMEM(x.shape, I32) for x in rows]
+        + buffers
         + [
             pltpu.VMEM((HALF_LANES, most), BF16),
             pltpu.VMEM((most, WIDTH), BF16),
@@ -398,7 +428,7 @@
             pltpu.VMEM((8, HALF_LANES), F32),
             pltpu.VMEM((HALF_LANES, 128), F32),
             pltpu.VMEM((8, WIDTH), F32),
-            dma((2,)),
+            dma((7,)),
             dma((2, MAIN)),
             dma((2, MAIN, 5)),
             dma((2, SMALL)),

time: 95.9 us -> 93.2 us (0.972)
  Pallas kernels: 93.7 us -> 91.2 us
    pallas_call x1, Pallas kernels: 93.7 us -> 91.2 us  [gather_multiply(): pl.pallas_call(kernel, out_shape=pltpu.VMEM((HALF, WIDTH), F32), in_specs...]
where the time goes in v3:
time: 93.2 us; the launch traced here: 93.1 us
  Pallas kernels  91.2 us (98%)
  local copies, waits for them, and re-layouts  1.94 us (2%)
    pallas_call x1, Pallas kernels, gather_multiply(): pl.pallas_call(kernel, out_shape=pltpu.VMEM((HALF, WIDTH), F32), in_specs...  91.2 us
    unnamed x1, local copies, waits for them, and re-layouts  1.94 us

profile of v3, /device:TPU:1, one launch (start us, length us, event | category | flops | bytes accessed | tf_op | source)
XLA Modules:
  0.0 93.1 jit_solution(9318245228657496041)
XLA Ops:
  0.0 91.2 %shard_map.73 = f32[704,1408]{1,0:T(8,128)S(1)} custom-call(f32[200,1408]{1,0:T(8,128)} %lam.1, f32[200,1408]{1,0:T(8,128)} %amp.1, s32[1200]{0:T(1024)} %virt_in.1, s32[704]{0:T(1024)} %ab_first_in.1, s32[704]{0:T(1024)} %ab_second_in.1, s32[1408]{0:T(1024)} %cd_first_in.1, s32[1408]{0:T(1024)} %cd_second_in.1), custom_call_target="tpu_custom_call" | custom-call | flops 19031654400 | bytes 8388608 | tf_op jit(solution)/shard_map/pallas_call | solution.py:416
  91.2 1.9 %copy.9 = f32[704,1408]{1,0:T(8,128)} copy(f32[704,1408]{1,0:T(8,128)S(1)} %shard_map.73) | data formatting | bytes 7929856

commit v4 on v3

--- a/solution.py
+++ b/solution.py
@@ -16,7 +16,6 @@
 LAST_ROWS = 16
 LAST_AT = (0, 2, 4, 7)
 LAST_SHARE, LAST_MULTIPLY = 9, 10
-SHARE_LAG = 3
 SOURCES = 8
 WIDTH = 1408
 HALF = 704
@@ -302,64 +301,19 @@
         mine = pl.ds(pl.multiple_of((HALF_LANES - HALF) * core, 64), HALF)
         out[...] += jnp.dot(left[mine, 0 : 3 * depth], right[0 : 3 * depth], preferred_element_type=F32)
 
-    def tick(t, _):
-        on_chunk(t + 2, lambda chunk: chunk.cross_own())
-        on_chunk(t + 1, lambda chunk: chunk.ring_own())
-        on_chunk(t, lambda chunk: chunk.ring_partner())
-        on_chunk(t, lambda chunk: chunk.pass_own())
-
-        @pl.when(t < CHUNKS)
-        def _():
-            on_chunk(t - 2, lambda chunk: chunk.pass_partner())
-
-        @pl.when(t == CHUNKS - 1)
-        def _():
-            for chunk in main(MAIN - 1):
-                chunk.pass_partner()
-
-        @pl.when(t == CHUNKS)
-        def _():
-            for chunk in small(SMALL - 1):
-                chunk.pass_partner()
-
-        @pl.when(t == 0)
-        def _():
-            for chunk in last:
-                chunk.pass_last()
-
-        for step, at in enumerate(LAST_AT):
-
-            @pl.when(t == at)
-            def _(step=step):
-                for chunk in last:
-                    chunk.cross_last(step)
-
-        @pl.when(t == LAST_SHARE)
-        def _():
-            for chunk in last:
-                for step in range(4):
-                    chunk.got(3 + step)
-            for copy in share_last():
-                copy.start()
-
-        @pl.when(t == LAST_MULTIPLY)
-        def _():
-            for copy in share_last():
-                copy.wait_recv()
-            multiply(lam_last, amp_last)
-
-        @pl.when((t >= SHARE_LAG) & (t < MAIN + SHARE_LAG))
-        def _():
-            j = t - SHARE_LAG
+    def on_kind(j, whole, half):
+        pl.when((j >= 0) & (j < MAIN))(lambda: whole(j))
+        pl.when((j >= MAIN) & (j < CHUNKS))(lambda: half(j - MAIN))
+
+    def hand_over(j):
+        def whole(j):
             for chunk in main(j):
                 chunk.got(3, 3)
                 chunk.got(4)
             for copy in share_main(j):
                 copy.start()
 
-        @pl.when((t >= MAIN + SHARE_LAG) & (t < CHUNKS + SHARE_LAG))
-        def _():
-            j = t - SHARE_LAG - MAIN
+        def half(j):
             for chunk in small(j):
                 chunk.got(3, 3)
             for copy in share_early(j):
@@ -369,9 +323,10 @@
             for copy in share_far(j):
                 copy.start()
 
-        @pl.when((t >= SHARE_LAG + 1) & (t < MAIN + SHARE_LAG + 1))
-        def _():
-            j = t - SHARE_LAG - 1
+        on_kind(j, whole, half)
+
+    def add_product(j):
+        def whole(j):
             for copy in share_main(j):
                 copy.wait_recv()
             multiply(lam_main.at[j], amp_main.at[j])
@@ -380,16 +335,63 @@
             for copy in share_main(j):
                 copy.wait_send()
 
-        @pl.when((t >= MAIN + SHARE_LAG + 1) & (t < CHUNKS + SHARE_LAG + 1))
-        def _():
-            j = t - SHARE_LAG - 1 - MAIN
+        def half(j):
             small_wait(j, small_core_recv.at[j, 0], 7)
             small_wait(j, small_core_recv.at[j, 1], 1)
             multiply(lam_small.at[j], amp_small.at[j])
 
+        on_kind(j, whole, half)
+
+    def tick(t, _):
+        on_chunk(t + 2, lambda chunk: chunk.cross_own())
+        on_chunk(t + 1, lambda chunk: chunk.ring_own())
+        on_chunk(t, lambda chunk: chunk.ring_partner())
+
+        @pl.when(t < CHUNKS)
+        def _():
+            hand_over(t - 3)
+
+        on_chunk(t, lambda chunk: chunk.pass_own())
+        on_chunk(t - 1, lambda chunk: chunk.pass_partner())
+
+        @pl.when(t == 0)
+        def _():
+            for chunk in last:
+                chunk.pass_last()
+
+        for step, at in enumerate(LAST_AT):
+
+            @pl.when(t == at)
+            def _(step=step):
+                for chunk in last:
+                    chunk.cross_last(step)
+
+        @pl.when(t == LAST_SHARE)
+        def _():
+            for chunk in last:
+                for step in range(4):
+                    chunk.got(3 + step)
+            for copy in share_last():
+                copy.start()
+
+        @pl.when(t == LAST_MULTIPLY)
+        def _():
+            for copy in share_last():
+                copy.wait_recv()
+            multiply(lam_last, amp_last)
+
+        @pl.when(t == CHUNKS)
+        def _():
+            hand_over(t - 3)
+
+        @pl.when(t >= CHUNKS)
+        def _():
+            hand_over(t - 2)
+
+        add_product(t - 3)
         return 0
 
-    lax.fori_loop(0, CHUNKS + SHARE_LAG + 1, tick, 0)
+    lax.fori_loop(0, CHUNKS + 3, tick, 0)
     for j in range(SMALL):
         for chunk in small(j):
             chunk.sent()

time: 93.2 us -> 92 us (0.987)
  Pallas kernels: 91.2 us -> 90 us
    pallas_call x1, Pallas kernels: 91.2 us -> 90 us  [gather_multiply(): pl.pallas_call(kernel, out_shape=pltpu.VMEM((HALF, WIDTH), F32), in_specs...]
where the time goes in v4:
time: 92 us; the launch traced here: 91.9 us
  Pallas kernels  90 us (98%)
  local copies, waits for them, and re-layouts  1.94 us (2%)
    pallas_call x1, Pallas kernels, gather_multiply(): pl.pallas_call(kernel, out_shape=pltpu.VMEM((HALF, WIDTH), F32), in_specs...  90 us
    unnamed x1, local copies, waits for them, and re-layouts  1.94 us

profile of v4, /device:TPU:1, one launch (start us, length us, event | category | flops | bytes accessed | tf_op | source)
XLA Modules:
  0.0 91.9 jit_solution(3997815990529566352)
XLA Ops:
  0.0 90.0 %shard_map.73 = f32[704,1408]{1,0:T(8,128)S(1)} custom-call(f32[200,1408]{1,0:T(8,128)} %lam.1, f32[200,1408]{1,0:T(8,128)} %amp.1, s32[1200]{0:T(1024)} %virt_in.1, s32[704]{0:T(1024)} %ab_first_in.1, s32[704]{0:T(1024)} %ab_second_in.1, s32[1408]{0:T(1024)} %cd_first_in.1, s32[1408]{0:T(1024)} %cd_second_in.1), custom_call_target="tpu_custom_call" | custom-call | flops 19031654400 | bytes 8388608 | tf_op jit(solution)/shard_map/pallas_call | solution.py:418
  90.0 1.9 %copy.9 = f32[704,1408]{1,0:T(8,128)} copy(f32[704,1408]{1,0:T(8,128)S(1)} %shard_map.73) | data formatting | bytes 7929856

commit v5 on v4

--- a/solution.py
+++ b/solution.py
@@ -380,11 +380,7 @@
                 copy.wait_recv()
             multiply(lam_last, amp_last)
 
-        @pl.when(t == CHUNKS)
-        def _():
-            hand_over(t - 3)
-
-        @pl.when(t >= CHUNKS)
+        @pl.when(t >= CHUNKS - 1)
         def _():
             hand_over(t - 2)
 

time: 92 us -> 90.9 us (0.988)
  Pallas kernels: 90 us -> 88.9 us
    pallas_call x1, Pallas kernels: 90 us -> 88.9 us  [gather_multiply(): pl.pallas_call(kernel, out_shape=pltpu.VMEM((HALF, WIDTH), F32), in_specs...]
where the time goes in v5:
time: 90.9 us; the launch traced here: 90.8 us
  Pallas kernels  88.9 us (98%)
  local copies, waits for them, and re-layouts  1.94 us (2%)
    pallas_call x1, Pallas kernels, gather_multiply(): pl.pallas_call(kernel, out_shape=pltpu.VMEM((HALF, WIDTH), F32), in_specs...  88.9 us
    unnamed x1, local copies, waits for them, and re-layouts  1.94 us

profile of v5, /device:TPU:1, one launch (start us, length us, event | category | flops | bytes accessed | tf_op | source)
XLA Modules:
  0.0 90.8 jit_solution(13313151118073985208)
XLA Ops:
  0.0 88.9 %shard_map.73 = f32[704,1408]{1,0:T(8,128)S(1)} custom-call(f32[200,1408]{1,0:T(8,128)} %lam.1, f32[200,1408]{1,0:T(8,128)} %amp.1, s32[1200]{0:T(1024)} %virt_in.1, s32[704]{0:T(1024)} %ab_first_in.1, s32[704]{0:T(1024)} %ab_second_in.1, s32[1408]{0:T(1024)} %cd_first_in.1, s32[1408]{0:T(1024)} %cd_second_in.1), custom_call_target="tpu_custom_call" | custom-call | flops 19031654400 | bytes 8388608 | tf_op jit(solution)/shard_map/pallas_call | solution.py:414
  88.9 1.9 %copy.9 = f32[704,1408]{1,0:T(8,128)} copy(f32[704,1408]{1,0:T(8,128)S(1)} %shard_map.73) | data formatting | bytes 7929856

commit v6 on v5

--- a/solution.py
+++ b/solution.py
@@ -14,8 +14,8 @@
 SMALL, SMALL_ROWS = 1, 8
 CHUNKS = MAIN + SMALL
 LAST_ROWS = 16
-LAST_AT = (0, 2, 4, 7)
-LAST_SHARE, LAST_MULTIPLY = 9, 10
+LAST_AT = (0, 2, 4, 6)
+LAST_SHARE, LAST_MULTIPLY = 8, 9
 SOURCES = 8
 WIDTH = 1408
 HALF = 704

time: 90.9 us -> 91.5 us (level)
  no operation moved by 1% of the time
where the time goes in v6:
time: 91.5 us; the launch traced here: 91.4 us
  Pallas kernels  89.4 us (98%)
  local copies, waits for them, and re-layouts  1.94 us (2%)
    pallas_call x1, Pallas kernels, gather_multiply(): pl.pallas_call(kernel, out_shape=pltpu.VMEM((HALF, WIDTH), F32), in_specs...  89.4 us
    unnamed x1, local copies, waits for them, and re-layouts  1.94 us

profile of v6, /device:TPU:1, one launch (start us, length us, event | category | flops | bytes accessed | tf_op | source)
XLA Modules:
  0.0 91.4 jit_solution(253179611854098337)
XLA Ops:
  0.0 89.4 %shard_map.73 = f32[704,1408]{1,0:T(8,128)S(1)} custom-call(f32[200,1408]{1,0:T(8,128)} %lam.1, f32[200,1408]{1,0:T(8,128)} %amp.1, s32[1200]{0:T(1024)} %virt_in.1, s32[704]{0:T(1024)} %ab_first_in.1, s32[704]{0:T(1024)} %ab_second_in.1, s32[1408]{0:T(1024)} %cd_first_in.1, s32[1408]{0:T(1024)} %cd_second_in.1), custom_call_target="tpu_custom_call" | custom-call | flops 19031654400 | bytes 8388608 | tf_op jit(solution)/shard_map/pallas_call | solution.py:414
  89.4 1.9 %copy.9 = f32[704,1408]{1,0:T(8,128)} copy(f32[704,1408]{1,0:T(8,128)S(1)} %shard_map.73) | data formatting | bytes 7929856
